TPU v7x, 512 devices: a whole 4x8x8 slice. The times are simulated.
512 devices in a mesh: gx: 64 (over z, y), gy: 8 (over x, core).
Axes of the slice: x: 4, y: 8, z: 8, core: 2. Of those that a mesh axis runs over, the one named last changes fastest.
Arguments:
- forward_coeff: float32 [192, 65536], P(None, ('gx', 'gy')), may hold values from -6 to 6
- incident: float32 [192, 65536], P(None, ('gx', 'gy')), may hold values from -6 to 6
- cost_grad: float32 [192, 65536], P(None, ('gx', 'gy')), may hold values from -6 to 6
- tmat_real: float32 [4, 96, 96], replicated, may hold values from -0.21875 to 0.21875
- tmat_imag: float32 [4, 96, 96], replicated, may hold values from -0.21875 to 0.21875
- translation_real: float32 [10, 96, 96], replicated, may hold values from -0.125 to 0.125
- translation_imaginary: float32 [10, 96, 96], replicated, may hold values from -0.125 to 0.125
- neighbours: int32 [10, 65536], P(None, ('gx', 'gy')), may hold values from -1 to 65535, as said below
- particle_type: int32 [65536], P(('gx', 'gy')), may hold values from 0 to 3
Outputs:
- adjoint: float32 [192, 65536], P(None, ('gx', 'gy'))
- sensitivity: float32 [4, 192, 192], replicated
Inputs may be any that keep to these rules, and one draw needn't show every extreme that they name: `neighbours`: particles sit on a lattice cut into spatial tiles of 4 rows (wide direction) by 32 columns (short direction); tile t holds slots t * 128 to t * 128 + 127, tiles numbered along the short direction fastest, and slot p of a tile sits at row p // 32 and column p % 32 of its tile. An entry of -1 marks an empty slot. Any other entry names a particle whose lattice row and column differ from the particle's own by dr and dc with 0 < dr^2 + dc^2 <= 5; the entries of one particle's list name distinct particles.
All inputs are finite; a program needn't handle non-finite values.
Results may differ from a plain program's by a relative error of at most 0.0001.
Values sent between devices are 32-bit elements; how exact they have to be, the bound alone decides.
No kernel may reach another device: no remote copies, remote signals or barrier semaphores. Data moves between devices by JAX's collectives and lax.ppermute only.
A program may use at most 64 MiB of HBM per device.

v0:
```python
import jax
import jax.numpy as jnp
from jax import lax
from jax.sharding import PartitionSpec as P

KRYLOV = 2
HIGH = lax.Precision.HIGHEST


def from_behind(block, axis, distance):
    devices = range(lax.axis_size(axis))
    route = [(i - distance, i) for i in devices if i - distance in devices]
    return lax.ppermute(block, axis, route)


def extended_2(x, sides, width):
    for axis, dim in sides:
        size, length = (lax.axis_size(axis), x.shape[dim])
        up = [(i, (i + 1) % size) for i in range(size - 1)]
        down = [(j, i) for i, j in up]
        last = lax.slice_in_dim(x, length - width, length, axis=dim)
        first = lax.slice_in_dim(x, 0, width, axis=dim)
        before = lax.ppermute(last, axis, up)
        after = lax.ppermute(first, axis, down)
        x = jnp.concatenate([before, x, after], axis=dim)
    return x


def complex_blocks(real_part, imag_part):
    upper_rows = jnp.concatenate([real_part, -imag_part], axis=2)
    lower_rows = jnp.concatenate([imag_part, real_part], axis=2)
    return jnp.concatenate([upper_rows, lower_rows], axis=1)


def small_solve(normal, right, steps):
    factor = jnp.linalg.cholesky(normal)
    forward_vals = []
    for row_index in range(steps):
        partial_sum = right[row_index]
        for col_index in range(row_index):
            partial_sum = partial_sum - factor[row_index, col_index] * forward_vals[col_index]
        forward_vals.append(partial_sum / factor[row_index, row_index])
    backward_vals = [None] * steps
    for row_index in reversed(range(steps)):
        partial_sum = forward_vals[row_index]
        for col_index in range(row_index + 1, steps):
            partial_sum = partial_sum - factor[col_index, row_index] * backward_vals[col_index]
        backward_vals[row_index] = partial_sum / factor[row_index, row_index]
    return backward_vals


def fold_wide(partial_value, dim):
    centre = jnp.take(partial_value, 1, axis=dim)
    for offset, piece in (
        (1, jnp.take(partial_value, 2, axis=dim)),
        (-1, jnp.take(partial_value, 0, axis=dim)),
    ):
        centre = centre + from_behind(piece, "gx", offset)
    return centre


def fold_short(partial_value, dim):
    centre = jnp.take(partial_value, 1, axis=dim)
    for offset, piece in (
        (1, jnp.take(partial_value, 2, axis=dim)),
        (-1, jnp.take(partial_value, 0, axis=dim)),
    ):
        centre = centre + from_behind(piece, "gy", offset)
    return centre


def body(
    forward_coeff,
    incident,
    cost_grad,
    tmat_real,
    tmat_imag,
    translation_real,
    translation_imaginary,
    neighbours,
    particle_type,
):
    width = forward_coeff.shape[0]
    local_count = forward_coeff.shape[1]
    kinds = tmat_real.shape[0]
    slots = translation_real.shape[0]
    steps = KRYLOV
    tmats = complex_blocks(tmat_real, tmat_imag)
    trans = complex_blocks(translation_real, translation_imaginary)
    tmat_stack = jnp.swapaxes(tmats, 1, 2).reshape(kinds * width, width)
    trans_adj = jnp.swapaxes(trans, 1, 2)
    kind_ids = jnp.arange(kinds, dtype=jnp.int32)
    type_mask = (particle_type[None, :] == kind_ids[:, None]).astype(jnp.float32)
    short_count = lax.axis_size("gy")
    tile = neighbours // local_count
    offset_x = tile // short_count - lax.axis_index("gx")
    offset_y = tile % short_count - lax.axis_index("gy")
    inner = neighbours % local_count
    target = (offset_x + 1) * (3 * local_count) + (offset_y + 1) * local_count + inner
    target = jnp.where(neighbours >= 0, target, 9 * local_count)
    flat_target = target.reshape(-1)
    extended = extended_2(
        forward_coeff.reshape(width, 1, 1, local_count), (("gx", 1), ("gy", 2)), 1
    )
    extended = jnp.concatenate(
        [extended.reshape(width, 9 * local_count), jnp.zeros((width, 1), jnp.float32)], axis=1
    )
    gathered = extended[:, target]
    exciting = incident + jnp.einsum("sdc,csp->dp", trans, gathered, precision=HIGH)
    beta = jnp.sqrt(lax.psum(jnp.sum(cost_grad * cost_grad), ("gx", "gy")))
    basis = [cost_grad / beta]
    columns = []
    for column in range(steps):
        vector = basis[column]
        all_kinds = jnp.dot(tmat_stack, vector, precision=HIGH).reshape(kinds, width, local_count)
        scaled = jnp.sum(type_mask[:, None, :] * all_kinds, axis=0)
        translated = jnp.einsum("sdc,cp->dsp", trans_adj, scaled, precision=HIGH).reshape(
            width, slots * local_count
        )
        collected = (
            jnp.zeros((width, 9 * local_count + 1), jnp.float32).at[:, flat_target].add(translated)
        )
        partial_value = collected[:, : 9 * local_count].reshape(width, 3, 3, local_count)
        summed = fold_short(fold_wide(partial_value, 1), 1)
        image = vector - summed
        local_dots = jnp.stack([jnp.sum(vec_item * image) for vec_item in basis])
        projections = lax.psum(local_dots, ("gx", "gy"))
        for row_index in range(column + 1):
            image = image - projections[row_index] * basis[row_index]
        height = jnp.sqrt(lax.psum(jnp.sum(image * image), ("gx", "gy")))
        columns.append(
            jnp.concatenate(
                [projections, height[None], jnp.zeros((steps - column - 1,), jnp.float32)]
            )
        )
        basis.append(image / height)
    hessen = jnp.stack(columns, axis=1)
    normal = jnp.dot(hessen.T, hessen, precision=HIGH)
    weights = small_solve(normal, beta * hessen[0], steps)
    adjoint = weights[0] * basis[0]
    column = 1
    adjoint = adjoint + weights[column] * basis[column]
    masked = adjoint[None, :, :] * type_mask[:, None, :]
    local_terms = jnp.einsum("kcp,dp->kcd", masked, exciting, precision=HIGH)
    sensitivity = lax.psum(local_terms, ("gx", "gy"))
    return (adjoint, sensitivity)


def solution(mesh):
    placed = (
        P(None, ("gx", "gy")),
        P(None, ("gx", "gy")),
        P(None, ("gx", "gy")),
        P(),
        P(),
        P(),
        P(),
        P(None, ("gx", "gy")),
        P(("gx", "gy")),
    )
    return jax.shard_map(
        body, mesh=mesh, in_specs=placed, out_specs=(P(None, ("gx", "gy")), P()), check_vma=False
    )
```

profile of v0, /device:TPU:23, one launch (start us, length us, event | category | flops | bytes accessed | tf_op | source)
XLA Modules:
  0.0 891.4 jit_solution(2647792898957183860)
XLA Ops:
  7.2 1.6 multiply_reduce_fusion.5
  8.8 102.0 %psum.42 = f32[]{:T(128)} all-reduce(f32[]{:T(128)} %multiply_reduce_fusion.5), channel_id=1, replica_groups=mesh['gx'=64,'gy'=8] {'gx','gy'}, use_global_device_ids=true, to_apply=%region_1.2 | all-reduce | flops 1 | bytes 8 | tf_op jit(solution)/shard_map/psum | solution.py:110
  114.8 1.8 fusion.10
  116.7 1.7 fusion.4
  119.2 8.3 scatter_custom_fusion
  127.9 4.7 collective-permute-start
  132.7 1.9 collective-permute-start.1
  134.8 3.9 collective-permute-done
  138.7 4.0 collective-permute-done.1
  142.8 1.4 collective-permute-start.2
  144.2 3.9 collective-permute-start.3
  149.8 100.7 %psum.43 = f32[1]{0:T(128)} all-reduce(f32[1]{0:T(128)} %bitcast.14), channel_id=1, replica_groups=mesh['gx'=64,'gy'=8] {'gx','gy'}, use_global_device_ids=true, to_apply=%region_5.12 | all-reduce | flops 1 | bytes 8 | tf_op jit(solution)/shard_map/psum | solution.py:127
  251.7 94.1 %psum.44 = f32[]{:T(128)} all-reduce(f32[]{:T(128)} %multiply_reduce_fusion.3), channel_id=1, replica_groups=mesh['gx'=64,'gy'=8] {'gx','gy'}, use_global_device_ids=true, to_apply=%region_7.14 | all-reduce | flops 1 | bytes 8 | tf_op jit(solution)/shard_map/psum | solution.py:130
  347.1 2.9 fusion.11
  350.0 1.7 fusion.7
  352.2 8.3 scatter_custom_fusion.1
  360.8 4.1 collective-permute-start.4
  365.8 1.9 collective-permute-start.5
  367.7 3.4 collective-permute-start.8
  371.1 1.9 collective-permute-start.9
  373.5 4.2 collective-permute-done.9
  379.0 4.4 collective-permute-start.11
  385.9 4.9 collective-permute-start.7
  391.4 4.1 gather_fusion
  395.5 1.6 multiply_reduce_fusion.2
  398.6 5.7 fusion.13
  404.3 98.6 %psum.45 = f32[2]{0:T(128)S(1)} all-reduce(f32[2]{0:T(128)S(1)} %pad_maximum_fusion.3), channel_id=1, replica_groups=mesh['gx'=64,'gy'=8] {'gx','gy'}, use_global_device_ids=true, to_apply=%region_12.19 | all-reduce | flops 2 | bytes 16 | tf_op jit(solution)/shard_map/psum | solution.py:127
  503.4 1.9 multiply_reduce_fusion
  506.1 94.3 %psum.46 = f32[]{:T(128)} all-reduce(f32[]{:T(128)} %multiply_reduce_fusion), channel_id=1, replica_groups=mesh['gx'=64,'gy'=8] {'gx','gy'}, use_global_device_ids=true, to_apply=%region_14.21 | all-reduce | flops 1 | bytes 8 | tf_op jit(solution)/shard_map/psum | solution.py:130
  609.3 1.7 fusion.18
  611.0 271.6 %all-reduce.3.cloned.1.call-done = f32[4,192,192]{2,1,0:T(8,128)} async-done(((f32[4,192,192]{2,1,0:T(8,128)}), f32[4,192,192]{2,1,0:T(8,128)}) %all-reduce.3.cloned.1.call-update) | async-done | bytes 589840 | tf_op jit(solution)/shard_map/psum | solution.py:145
  882.5 2.1 copy.46
  (98 shorter events, 20.3 us)
Async XLA Ops:
  7.2 107.4 %copy-start.1 = (f32[10,96,96]{2,1,0:T(8,128)S(1)}, f32[10,96,96]{2,1,0:T(8,128)}, u32[]{:S(2)}) copy-start(f32[10,96,96]{2,1,0:T(8,128)} %param.26) | copy-start | bytes 1105924
  7.2 875.4 %all-reduce.3.cloned.1.call-start = ((), (), s32[]{:S(2)}) async-start(), calls=%async_computation | async-start | bytes 1572864 | tf_op jit(solution)/shard_map/psum | solution.py:145
  112.2 234.9 %copy-start.14 = (f32[4,128]{1,0:T(4,128)}, f32[4,128]{1,0:T(4,128)S(1)}, u32[]{:S(2)}) copy-start(f32[4,128]{1,0:T(4,128)S(1)} %fusion.51) | copy-start | bytes 6148
  113.1 1.7 copy-start.12
  113.1 1.7 copy-start
  113.2 1.7 copy-start.10
  113.2 1.7 copy-start.17
  114.6 2.1 copy-start.2
  114.8 3.6 copy-start.5
  118.5 0.7 copy-start.16
  127.9 10.8 %collective-permute-start = (f32[192,3,128]{2,0,1:T(8,128)S(1)}, f32[192,3,128]{2,0,1:T(8,128)S(1)}, u32[]{:S(2)}, u32[]{:S(2)}) collective-permute-start(f32[192,3,128]{2,0,1:T(8,128)S(1)} %bitcast.131), channel_id=1, source_target_pairs={{0,8},{8,16},{16,24},{24,32},{32,40},{40,48},{48,56},{56,64},{64,7... | collective-permute-start | bytes 884744 | tf_op jit(solution)/shard_map/ppermute | solution.py:13
  132.7 9.9 %collective-permute-start.1 = (f32[192,3,128]{2,0,1:T(8,128)S(1)}, f32[192,3,128]{2,0,1:T(8,128)S(1)}, u32[]{:S(2)}, u32[]{:S(2)}) collective-permute-start(f32[192,3,128]{2,0,1:T(8,128)S(1)} %bitcast.132), channel_id=1, source_target_pairs={{8,0},{16,8},{24,16},{32,24},{40,32},{48,40},{56,48},{64,56},{72,6... | collective-permute-start | bytes 884744 | tf_op jit(solution)/shard_map/ppermute | solution.py:13
  134.8 212.3 %copy-start.11 = (f32[4,96,96]{2,1,0:T(8,128)S(1)}, f32[4,96,96]{2,1,0:T(8,128)}, u32[]{:S(2)}) copy-start(f32[4,96,96]{2,1,0:T(8,128)} %param.25) | copy-start | bytes 442372
  134.8 212.3 %copy-start.13 = (f32[4,96,96]{2,1,0:T(8,128)S(1)}, f32[4,96,96]{2,1,0:T(8,128)}, u32[]{:S(2)}) copy-start(f32[4,96,96]{2,1,0:T(8,128)} %copy-done.12) | copy-start | bytes 442372
  142.7 207.2 %copy-start.3 = (f32[10,96,96]{1,2,0:T(8,128)S(1)}, f32[10,96,96]{1,2,0:T(8,128)}, u32[]{:S(2)}) copy-start(f32[10,96,96]{1,2,0:T(8,128)} %copy-done.2) | copy-start | bytes 1105924
  142.7 207.2 %copy-start.6 = (f32[10,96,96]{1,2,0:T(8,128)S(1)}, f32[10,96,96]{1,2,0:T(8,128)}, u32[]{:S(2)}) copy-start(f32[10,96,96]{1,2,0:T(8,128)} %copy-done.5) | copy-start | bytes 1105924
  142.8 5.4 collective-permute-start.2
  144.2 4.8 collective-permute-start.3
  360.5 7.2 copy-start.8
  360.8 22.8 %collective-permute-start.4 = (f32[192,3,128]{2,0,1:T(8,128)S(1)}, f32[192,3,128]{2,0,1:T(8,128)S(1)}, u32[]{:S(2)}, u32[]{:S(2)}) collective-permute-start(f32[192,3,128]{2,0,1:T(8,128)S(1)} %bitcast.130), channel_id=1, source_target_pairs={{0,8},{8,16},{16,24},{24,32},{32,40},{40,48},{48,56},{56,64},{64,7... | collective-permute-start | bytes 884744 | tf_op jit(solution)/shard_map/ppermute | solution.py:13
  365.8 17.8 %collective-permute-start.5 = (f32[192,3,128]{2,0,1:T(8,128)}, f32[192,3,128]{2,0,1:T(8,128)}, u32[]{:S(2)}, u32[]{:S(2)}) collective-permute-start(f32[192,3,128]{2,0,1:T(8,128)} %bitcast.26), channel_id=1, source_target_pairs={{8,0},{16,8},{24,16},{32,24},{40,32},{48,40},{56,48},{64,56},{72,6... | collective-permute-start | bytes 884744 | tf_op jit(solution)/shard_map/ppermute | solution.py:13
  367.7 5.8 collective-permute-start.8
  371.1 6.6 collective-permute-start.9
  377.7 13.2 %collective-permute-start.10 = (f32[192,3,1,128]{3,0,2,1:T(8,128)S(1)}, f32[192,3,1,128]{3,0,2,1:T(8,128)S(1)}, u32[]{:S(2)}, u32[]{:S(2)}) collective-permute-start(f32[192,3,1,128]{3,0,2,1:T(8,128)S(1)} %pad_maximum_fusion.1), channel_id=1, source_target_pairs={{0,1},{1,2},{2,3},{3,4},{4,5},{5,6},{6,7},{8,9},{9,10},{10,11},{11... | collective-permute-start | bytes 884744 | tf_op jit(solution)/shard_map/ppermute | solution.py:23
  379.0 11.9 %collective-permute-start.11 = (f32[192,3,1,128]{3,0,2,1:T(8,128)S(1)}, f32[192,3,1,128]{3,0,2,1:T(8,128)S(1)}, u32[]{:S(2)}, u32[]{:S(2)}) collective-permute-start(f32[192,3,1,128]{3,0,2,1:T(8,128)S(1)} %pad_maximum_fusion.1), channel_id=1, source_target_pairs={{1,0},{2,1},{3,2},{4,3},{5,4},{6,5},{7,6},{9,8},{10,9},{11,10},{12... | collective-permute-start | bytes 884744 | tf_op jit(solution)/shard_map/ppermute | solution.py:24
  384.6 10.9 %collective-permute-start.6 = (f32[192,128]{1,0:T(8,128)S(1)}, f32[192,128]{1,0:T(8,128)}, u32[]{:S(2)}, u32[]{:S(2)}) collective-permute-start(f32[192,128]{1,0:T(8,128)S(1)} %get-tuple-element.87), channel_id=1, source_target_pairs={{0,1},{1,2},{2,3},{3,4},{4,5},{5,6},{6,7},{8,9},{9,10},{10,11},{11... | collective-permute-start | bytes 294920 | tf_op jit(solution)/shard_map/ppermute | solution.py:13
  385.9 9.6 %collective-permute-start.7 = (f32[192,128]{1,0:T(8,128)S(1)}, f32[192,128]{1,0:T(8,128)}, u32[]{:S(2)}, u32[]{:S(2)}) collective-permute-start(f32[192,128]{1,0:T(8,128)S(1)} %get-tuple-element.88), channel_id=1, source_target_pairs={{1,0},{2,1},{3,2},{4,3},{5,4},{6,5},{7,6},{9,8},{10,9},{11,10},{12... | collective-permute-start | bytes 294920 | tf_op jit(solution)/shard_map/ppermute | solution.py:13
  391.4 7.2 copy-start.4
  391.4 7.2 copy-start.7
  391.4 7.2 copy-start.18
  398.6 210.7 %copy-start.15 = (f32[4,128]{1,0:T(4,128)S(1)}, f32[4,128]{1,0:T(4,128)}, u32[]{:S(2)}) copy-start(f32[4,128]{1,0:T(4,128)} %copy-done.14) | copy-start | bytes 6148
  609.2 275.3 %copy-start.9 = (f32[192,128]{1,0:T(8,128)}, f32[192,128]{1,0:T(8,128)S(1)}, u32[]{:S(2)}) copy-start(f32[192,128]{1,0:T(8,128)S(1)} %multiply_add_fusion) | copy-start | bytes 294916
Sparse Core Ops, SparseCore 0:
  611.1 271.3 all-reduce.2
where the time goes:
time: 893 us; the launch traced here: 891 us
  blocking collectives  490 us (55%)
  waiting for transfers between devices  285 us (32%)
  starting transfers between devices  35.2 us (4%)
  other arithmetic  30.8 us (3%)
  between operations  21.8 us (2%)
  matrix products  15.7 us (2%)
  local copies, waits for them, and re-layouts  13.2 us (1%)
    psum x1, waiting for transfers between devices, body(): sensitivity = lax.psum(local_terms, ('gx', 'gy'))  272 us
    psum x2, blocking collectives, body(): projections = lax.psum(local_dots, ('gx', 'gy'))  199 us
    psum x2, blocking collectives, body(): height = jnp.sqrt(lax.psum(jnp.sum(image * image), ('gx', 'gy')))  188 us
    psum x1, blocking collectives, body(): beta = jnp.sqrt(lax.psum(jnp.sum(cost_grad * cost_grad), ('gx', 'gy')))  102 us
    ppermute x8, starting transfers between devices, from_behind(): return lax.ppermute(block, axis, route)  24.1 us
  transfers between devices with their start and end apart: 13, of which 6 were waited for; matrix products, arithmetic and copies ran while one was open for 1% of the time, Pallas kernels for 0%

commit v1 on v0

--- a/solution.py
+++ b/solution.py
@@ -124,7 +124,9 @@
         summed = fold_short(fold_wide(partial_value, 1), 1)
         image = vector - summed
         local_dots = jnp.stack([jnp.sum(vec_item * image) for vec_item in basis])
-        projections = lax.psum(local_dots, ("gx", "gy"))
+        projections = local_dots
+        for mesh_axis in ("gy", "gx"):
+            projections = lax.psum(projections, mesh_axis)
         for row_index in range(column + 1):
             image = image - projections[row_index] * basis[row_index]
         height = jnp.sqrt(lax.psum(jnp.sum(image * image), ("gx", "gy")))

time: 893 us -> 1010 us (1.13)
  blocking collectives: 490 us -> 608 us
    psum x2, blocking collectives: 188 us -> 259 us  [body(): height = jnp.sqrt(lax.psum(jnp.sum(image * image), ('gx', 'gy')))]
    psum x2 -> x4, blocking collectives: 199 us -> 246 us  [body(): projections = lax.psum(projections, mesh_axis)]
  transfers between devices with their start and end apart: 13 -> 13, of which waited for: 6 -> 6; matrix products, arithmetic and copies ran while one was open for 1% -> 0% of each run, Pallas kernels for 0% -> 0%
where the time goes in v1:
time: 1010 us
  blocking collectives  608 us (60%)
  waiting for transfers between devices  286 us (28%)
  starting transfers between devices  35.1 us (3%)
  other arithmetic  31.3 us (3%)
  between operations  21.9 us (2%)
  matrix products  14.8 us (1%)
  local copies, waits for them, and re-layouts  12.3 us (1%)
    psum x1, waiting for transfers between devices, body(): sensitivity = lax.psum(local_terms, ('gx', 'gy'))  272 us
    psum x2, blocking collectives, body(): height = jnp.sqrt(lax.psum(jnp.sum(image * image), ('gx', 'gy')))  259 us
    psum x4, blocking collectives, body(): projections = lax.psum(projections, mesh_axis)  246 us
    psum x1, blocking collectives, body(): beta = jnp.sqrt(lax.psum(jnp.sum(cost_grad * cost_grad), ('gx', 'gy')))  102 us
    ppermute x8, starting transfers between devices, from_behind(): return lax.ppermute(block, axis, route)  24.5 us
  transfers between devices with their start and end apart: 13, of which 6 were waited for; matrix products, arithmetic and copies ran while one was open for 0% of the time, Pallas kernels for 0%

profile of v1, /device:TPU:23, one launch (start us, length us, event | category | flops | bytes accessed | tf_op | source)
XLA Modules:
  0.0 1009.1 jit_solution(16436459287751784827)
XLA Ops:
  8.8 102.0 %psum.56 = f32[]{:T(128)} all-reduce(f32[]{:T(128)} %multiply_reduce_fusion.5), channel_id=1, replica_groups=mesh['gx'=64,'gy'=8] {'gx','gy'}, use_global_device_ids=true, to_apply=%region_1.2 | all-reduce | flops 1 | bytes 8 | tf_op jit(solution)/shard_map/psum | solution.py:110
  114.8 1.8 fusion.10
  116.7 1.7 fusion.4
  119.2 8.3 scatter_custom_fusion
  127.9 4.7 collective-permute-start
  132.7 1.9 collective-permute-start.1
  134.8 3.9 collective-permute-done
  138.7 4.0 collective-permute-done.1
  144.2 3.9 collective-permute-start.3
  149.7 15.6 %psum.57 = f32[1]{0:T(128)} all-reduce(f32[1]{0:T(128)} %bitcast.14), channel_id=1, replica_groups=mesh['gx'=64,'gy'=8] {'gy'}, use_global_device_ids=true, to_apply=%region_5.12 | all-reduce | flops 1 | bytes 8 | tf_op jit(solution)/shard_map/psum | solution.py:129
  165.2 107.8 %psum.58 = f32[1]{0:T(128)} all-reduce(f32[1]{0:T(128)} %psum.57), channel_id=1, replica_groups=mesh['gx'=64,'gy'=8] {'gx'}, use_global_device_ids=true, to_apply=%region_6.13 | all-reduce | flops 1 | bytes 8 | tf_op jit(solution)/shard_map/psum | solution.py:129
  274.3 126.4 %psum.59 = f32[]{:T(128)} all-reduce(f32[]{:T(128)} %multiply_reduce_fusion.3), channel_id=1, replica_groups=mesh['gx'=64,'gy'=8] {'gx','gy'}, use_global_device_ids=true, to_apply=%region_8.15 | all-reduce | flops 1 | bytes 8 | tf_op jit(solution)/shard_map/psum | solution.py:132
  402.1 1.8 fusion.11
  404.0 1.7 fusion.7
  406.1 8.3 scatter_custom_fusion.1
  414.8 4.3 collective-permute-start.4
  420.0 2.1 collective-permute-start.5
  422.1 3.2 collective-permute-start.8
  425.3 2.1 collective-permute-start.9
  428.0 4.2 collective-permute-done.9
  433.6 3.9 collective-permute-start.11
  440.0 4.9 collective-permute-start.7
  445.5 2.2 multiply_reduce_fusion.2
  449.0 3.1 gather_fusion
  452.2 15.0 %psum.60 = f32[2]{0:T(128)S(1)} all-reduce(f32[2]{0:T(128)S(1)} %pad_maximum_fusion.3), channel_id=1, replica_groups=mesh['gx'=64,'gy'=8] {'gy'}, use_global_device_ids=true, to_apply=%region_13.20 | all-reduce | flops 2 | bytes 16 | tf_op jit(solution)/shard_map/psum | solution.py:129
  467.2 5.8 fusion.13
  473.0 108.1 %psum.61 = f32[2]{0:T(128)S(1)} all-reduce(f32[2]{0:T(128)S(1)} %psum.60), channel_id=1, replica_groups=mesh['gx'=64,'gy'=8] {'gx'}, use_global_device_ids=true, to_apply=%region_14.21 | all-reduce | flops 2 | bytes 16 | tf_op jit(solution)/shard_map/psum | solution.py:129
  581.7 2.0 multiply_reduce_fusion
  584.4 133.1 %psum.62 = f32[]{:T(128)} all-reduce(f32[]{:T(128)} %multiply_reduce_fusion), channel_id=1, replica_groups=mesh['gx'=64,'gy'=8] {'gx','gy'}, use_global_device_ids=true, to_apply=%region_16.23 | all-reduce | flops 1 | bytes 8 | tf_op jit(solution)/shard_map/psum | solution.py:132
  726.4 1.7 fusion.18
  728.1 272.1 %all-reduce.3.cloned.1.call-done = f32[4,192,192]{2,1,0:T(8,128)} async-done(((f32[4,192,192]{2,1,0:T(8,128)}), f32[4,192,192]{2,1,0:T(8,128)}) %all-reduce.3.cloned.1.call-update) | async-done | bytes 589840 | tf_op jit(solution)/shard_map/psum | solution.py:147
  1000.2 2.1 copy.46
  (98 shorter events, 23.3 us)
Async XLA Ops:
  7.2 107.4 %copy-start.1 = (f32[10,96,96]{2,1,0:T(8,128)S(1)}, f32[10,96,96]{2,1,0:T(8,128)}, u32[]{:S(2)}) copy-start(f32[10,96,96]{2,1,0:T(8,128)} %param.26) | copy-start | bytes 1105924
  7.2 993.0 %all-reduce.3.cloned.1.call-start = ((), (), s32[]{:S(2)}) async-start(), calls=%async_computation | async-start | bytes 1572864 | tf_op jit(solution)/shard_map/psum | solution.py:147
  112.2 289.9 %copy-start.13 = (f32[4,128]{1,0:T(4,128)}, f32[4,128]{1,0:T(4,128)S(1)}, u32[]{:S(2)}) copy-start(f32[4,128]{1,0:T(4,128)S(1)} %fusion.51) | copy-start | bytes 6148
  113.1 1.7 copy-start.11
  113.1 1.7 copy-start
  113.1 1.7 copy-start.9
  113.2 1.7 copy-start.16
  114.6 2.1 copy-start.2
  114.8 3.6 copy-start.4
  118.4 0.7 copy-start.15
  127.9 10.8 %collective-permute-start = (f32[192,3,128]{2,0,1:T(8,128)S(1)}, f32[192,3,128]{2,0,1:T(8,128)S(1)}, u32[]{:S(2)}, u32[]{:S(2)}) collective-permute-start(f32[192,3,128]{2,0,1:T(8,128)S(1)} %bitcast.131), channel_id=1, source_target_pairs={{0,8},{8,16},{16,24},{24,32},{32,40},{40,48},{48,56},{56,64},{64,7... | collective-permute-start | bytes 884744 | tf_op jit(solution)/shard_map/ppermute | solution.py:13
  132.7 9.9 collective-permute-start.1
  134.8 267.3 %copy-start.10 = (f32[4,96,96]{2,1,0:T(8,128)S(1)}, f32[4,96,96]{2,1,0:T(8,128)}, u32[]{:S(2)}) copy-start(f32[4,96,96]{2,1,0:T(8,128)} %param.25) | copy-start | bytes 442372
  134.8 267.3 %copy-start.12 = (f32[4,96,96]{2,1,0:T(8,128)S(1)}, f32[4,96,96]{2,1,0:T(8,128)}, u32[]{:S(2)}) copy-start(f32[4,96,96]{2,1,0:T(8,128)} %copy-done.11) | copy-start | bytes 442372
  134.8 267.3 %copy-start.17 = (f32[4,96,96]{2,1,0:T(8,128)S(1)}, f32[4,96,96]{2,1,0:T(8,128)}, u32[]{:S(2)}) copy-start(f32[4,96,96]{2,1,0:T(8,128)} %param.24) | copy-start | bytes 442372
  142.7 261.2 %copy-start.3 = (f32[10,96,96]{1,2,0:T(8,128)S(1)}, f32[10,96,96]{1,2,0:T(8,128)}, u32[]{:S(2)}) copy-start(f32[10,96,96]{1,2,0:T(8,128)} %copy-done.2) | copy-start | bytes 1105924
  142.7 261.2 %copy-start.5 = (f32[10,96,96]{1,2,0:T(8,128)S(1)}, f32[10,96,96]{1,2,0:T(8,128)}, u32[]{:S(2)}) copy-start(f32[10,96,96]{1,2,0:T(8,128)} %copy-done.4) | copy-start | bytes 1105924
  142.8 5.4 collective-permute-start.2
  144.2 4.8 collective-permute-start.3
  414.5 7.6 copy-start.6
  414.8 22.9 %collective-permute-start.4 = (f32[192,3,128]{2,0,1:T(8,128)S(1)}, f32[192,3,128]{2,0,1:T(8,128)S(1)}, u32[]{:S(2)}, u32[]{:S(2)}) collective-permute-start(f32[192,3,128]{2,0,1:T(8,128)S(1)} %bitcast.130), channel_id=1, source_target_pairs={{0,8},{8,16},{16,24},{24,32},{32,40},{40,48},{48,56},{56,64},{64,7... | collective-permute-start | bytes 884744 | tf_op jit(solution)/shard_map/ppermute | solution.py:13
  420.0 17.7 %collective-permute-start.5 = (f32[192,3,128]{2,0,1:T(8,128)}, f32[192,3,128]{2,0,1:T(8,128)}, u32[]{:S(2)}, u32[]{:S(2)}) collective-permute-start(f32[192,3,128]{2,0,1:T(8,128)} %bitcast.26), channel_id=1, source_target_pairs={{8,0},{16,8},{24,16},{32,24},{40,32},{48,40},{56,48},{64,56},{72,6... | collective-permute-start | bytes 884744 | tf_op jit(solution)/shard_map/ppermute | solution.py:13
  422.1 5.9 collective-permute-start.8
  425.3 6.9 collective-permute-start.9
  432.3 12.6 %collective-permute-start.10 = (f32[192,3,1,128]{3,0,2,1:T(8,128)S(1)}, f32[192,3,1,128]{3,0,2,1:T(8,128)S(1)}, u32[]{:S(2)}, u32[]{:S(2)}) collective-permute-start(f32[192,3,1,128]{3,0,2,1:T(8,128)S(1)} %pad_maximum_fusion.1), channel_id=1, source_target_pairs={{0,1},{1,2},{2,3},{3,4},{4,5},{5,6},{6,7},{8,9},{9,10},{10,11},{11... | collective-permute-start | bytes 884744 | tf_op jit(solution)/shard_map/ppermute | solution.py:23
  433.6 11.3 %collective-permute-start.11 = (f32[192,3,1,128]{3,0,2,1:T(8,128)S(1)}, f32[192,3,1,128]{3,0,2,1:T(8,128)S(1)}, u32[]{:S(2)}, u32[]{:S(2)}) collective-permute-start(f32[192,3,1,128]{3,0,2,1:T(8,128)S(1)} %pad_maximum_fusion.1), channel_id=1, source_target_pairs={{1,0},{2,1},{3,2},{4,3},{5,4},{6,5},{7,6},{9,8},{10,9},{11,10},{12... | collective-permute-start | bytes 884744 | tf_op jit(solution)/shard_map/ppermute | solution.py:24
  438.7 6.7 collective-permute-start.6
  440.0 5.4 collective-permute-start.7
  467.2 114.5 %copy-start.7 = (f32[192,128]{1,0:T(8,128)S(1)}, f32[192,128]{1,0:T(8,128)}, u32[]{:S(2)}) copy-start(f32[192,128]{1,0:T(8,128)} %get-tuple-element.78) | copy-start | bytes 294916
  467.2 259.2 %copy-start.14 = (f32[4,128]{1,0:T(4,128)S(1)}, f32[4,128]{1,0:T(4,128)}, u32[]{:S(2)}) copy-start(f32[4,128]{1,0:T(4,128)} %copy-done.13) | copy-start | bytes 6148
  726.4 275.9 %copy-start.8 = (f32[192,128]{1,0:T(8,128)}, f32[192,128]{1,0:T(8,128)S(1)}, u32[]{:S(2)}) copy-start(f32[192,128]{1,0:T(8,128)S(1)} %multiply_add_fusion) | copy-start | bytes 294916
Sparse Core Ops, SparseCore 0:
  728.2 271.8 all-reduce.2
